TPU v7x, 32 devices: a whole 2x2x4 slice. The times are simulated.
32 devices in a mesh: ens: 2 (over y), ta: 4 (over z), gz: 2 (over x), gy: 2 (over core).
Axes of the slice: x: 2, y: 2, z: 4, core: 2. Of those that a mesh axis runs over, the one named last changes fastest.
Arguments:
- raw_links: float32 [8, 3, 3, 2, 8, 4, 256], P('ens', None, None, None, 'ta', 'gz', 'gy'), parts along dimension 0, may hold values from -0.25 to 1.25, as said below
Outputs:
- relaxed_links: float32 [8, 3, 3, 2, 8, 4, 256], P('ens', None, None, None, 'ta', 'gz', 'gy'), parts along dimension 0
There are 2 independent parts, one for each index of `ens`. A program takes and returns all parts, laid end to end along the dimension named above; each array names one. Nothing has to cross between parts.
Inputs may be any that keep to these rules, and one draw needn't show every extreme that they name: `raw_links`: each real entry lies within 0.25 of the corresponding entry of the identity matrix.
All inputs are finite; a program needn't handle non-finite values.
Results may differ from a plain program's by a relative error of at most 0.0003.
Values sent between devices are 32-bit elements; how exact they have to be, the bound alone decides.
A program may use at most 64 MiB of HBM per device.

v0:
```python
import functools

import jax
import jax.numpy as jnp
from jax import lax
from jax.experimental import pallas as pl
from jax.experimental.pallas import tpu as pltpu
from jax.sharding import PartitionSpec as P

X = 16
LANES = 128
MESH = pl.DeviceIdType.MESH


def product(a, b, a_dagger=False, b_dagger=False):
    depth = a[0].shape[0] if a_dagger else a[0].shape[1]
    real = imag = None
    for k in range(depth):
        left = [(part[k] if a_dagger else part[:, k])[:, None] for part in a]
        right = [(part[:, k] if b_dagger else part[k])[None] for part in b]
        if a_dagger != b_dagger:
            real_term = left[0] * right[0] + left[1] * right[1]
            if a_dagger:
                imag_term = left[0] * right[1] - left[1] * right[0]
            else:
                imag_term = left[1] * right[0] - left[0] * right[1]
        else:
            real_term = left[0] * right[0] - left[1] * right[1]
            imag_term = left[0] * right[1] + left[1] * right[0]
        real = real_term if real is None else real + real_term
        imag = imag_term if imag is None else imag + imag_term
    return real, imag


def third(real, imag):
    rows = []
    for j in range(3):
        k, m = (j + 1) % 3, (j + 2) % 3
        a_r, a_i, b_r, b_i = real[0, k], imag[0, k], real[1, m], imag[1, m]
        c_r, c_i, d_r, d_i = real[0, m], imag[0, m], real[1, k], imag[1, k]
        rows.append(
            (
                (a_r * b_r - a_i * b_i) - (c_r * d_r - c_i * d_i),
                (c_r * d_i + c_i * d_r) - (a_r * b_i + a_i * b_r),
            )
        )
    return jnp.stack([r for r, _ in rows]), jnp.stack([i for _, i in rows])


def closed(pair):
    real, imag = pair
    last_r, last_i = third(real, imag)
    return (
        jnp.concatenate([real, last_r[None]], axis=0),
        jnp.concatenate([imag, last_i[None]], axis=0),
    )


def two_rows(pair):
    return pair[0][:2], pair[1][:2]


def two_columns(pair):
    return pair[0][:, :2], pair[1][:, :2]


def plus(a, b):
    return a[0] + b[0], a[1] + b[1]


def roll(value, shift, axis):
    return pltpu.roll(value, shift % value.shape[axis], axis)


def project(rows):
    lead, second = rows[0], rows[1]
    square = lead * lead
    norm = square[0, 0] + square[0, 1] + square[1, 0] + square[1, 1] + square[2, 0] + square[2, 1]
    lead = lead * (1.0 / jnp.sqrt(norm))[None, None]
    cr = ci = None
    for j in range(3):
        r = lead[j, 0] * second[j, 0] + lead[j, 1] * second[j, 1]
        i = lead[j, 0] * second[j, 1] - lead[j, 1] * second[j, 0]
        cr = r if cr is None else cr + r
        ci = i if ci is None else ci + i
    new = []
    norm = None
    for j in range(3):
        r = second[j, 0] - (cr * lead[j, 0] - ci * lead[j, 1])
        i = second[j, 1] - (cr * lead[j, 1] + ci * lead[j, 0])
        new.append((r, i))
        norm = r * r + i * i if norm is None else norm + (r * r + i * i)
    inverse = 1.0 / jnp.sqrt(norm)
    lead = [(lead[j, 0], lead[j, 1]) for j in range(3)]
    return [lead, [(r * inverse, i * inverse) for r, i in new]]


def reflect(link, staple):
    w_r, w_i = product(link, staple)
    w = {(i, j): (w_r[i, j], w_i[i, j]) for i in range(3) for j in range(3)}
    u = {i: (link[0][i], link[1][i]) for i in range(3)}
    needed = {(0, 1): ((0, 1, 2), (1, 2)), (0, 2): ((), (1, 2)), (1, 2): ((), ())}
    for a, b in ((0, 1), (0, 2), (1, 2)):
        q0 = 0.5 * (w[a, a][0] + w[b, b][0])
        q1 = 0.5 * (w[a, b][1] + w[b, a][1])
        q2 = 0.5 * (w[a, b][0] - w[b, a][0])
        q3 = 0.5 * (w[a, a][1] - w[b, b][1])
        vector = q1 * q1 + q2 * q2 + q3 * q3
        square = q0 * q0
        inverse = 1.0 / (square + vector)
        c0 = (square - vector) * inverse
        scale = -2.0 * q0 * inverse
        c1, c2, c3 = scale * q1, scale * q2, scale * q3

        def first(top, low):
            return (
                (c0 * top[0] - c3 * top[1]) + (c2 * low[0] - c1 * low[1]),
                (c0 * top[1] + c3 * top[0]) + (c2 * low[1] + c1 * low[0]),
            )

        def last(top, low):
            return (
                (c0 * low[0] + c3 * low[1]) - (c2 * top[0] + c1 * top[1]),
                (c0 * low[1] - c3 * low[0]) + (c1 * top[0] - c2 * top[1]),
            )

        u[a], u[b] = first(u[a], u[b]), last(u[a], u[b])
        tops, lows = needed[a, b]
        new = {(a, j): first(w[a, j], w[b, j]) for j in tops}
        new.update({(b, j): last(w[a, j], w[b, j]) for j in lows})
        w.update(new)
    return jnp.stack([u[i][0] for i in range(3)]), jnp.stack([u[i][1] for i in range(3)])


def kernel(
    counts,
    x_ref,
    o_ref,
    raw,
    packed,
    gathered,
    rim,
    link_r,
    link_i,
    rim_r,
    rim_i,
    up_out,
    up_in,
    down_out,
    down_in,
    natural,
    load_sem,
    own_sem,
    sib_send,
    sib_recv,
    gz_send,
    gz_recv,
    fwd_send,
    fwd_recv,
    rim_send,
    rim_recv,
    rfw_send,
    rfw_recv,
    up_send,
    up_recv,
    down_send,
    down_recv,
    store_sem,
):
    ta_n, gz_n, t_len, z_len = counts
    piece = t_len * z_len
    rows = gz_n * piece
    ta, gz, gy = lax.axis_index("ta"), lax.axis_index("gz"), lax.axis_index("gy")
    later, earlier = lax.rem(ta + 1, ta_n), lax.rem(ta + ta_n - 1, ta_n)
    sibling = {"gy": 1 - gy}

    def side(k):
        return lax.rem(gz + k, gz_n)

    def behind(k):
        return lax.rem(gz + gz_n - k, gz_n)

    loads = []
    for half in range(2):
        for z in range(z_len):
            for t in range(t_len):
                row = half * piece + z * t_len + t
                loads.append(
                    pltpu.make_async_copy(
                        x_ref.at[2 * half : 2 * half + 2, 0:2, :, :, t, z, :],
                        raw.at[:, :, :, :, row, :],
                        load_sem.at[row],
                    )
                )
    for copy in loads:
        copy.start()

    barrier = pltpu.get_barrier_semaphore()
    greeted = [sibling] + [{"gz": side(k)} for k in range(1, gz_n)]
    for k in range(gz_n):
        greeted.append({"ta": later, "gz": side(k)})
        greeted.append({"ta": earlier, "gz": side(k)})
    for device in greeted:
        pl.semaphore_signal(barrier, inc=1, device_id=device, device_id_type=MESH)

    for copy in loads:
        copy.wait()

    small = (2 * piece, LANES)
    row_id = lax.broadcasted_iota(jnp.int32, small, 0)
    lane_id = lax.broadcasted_iota(jnp.int32, small, 1)
    inner = row_id % piece
    place = lane_id % 64
    odd = (inner // t_len + inner % t_len + place // 8 + lane_id // 64) % 2
    pick = (place // 8) * X + 2 * (place % 8) + odd
    for pair in range(2):
        for i, row in enumerate(project(raw[pair])):
            for j, entry in enumerate(row):
                for c in range(2):
                    packed[pair, i, j, c] = jnp.take_along_axis(entry[c], pick, axis=1)

    pl.semaphore_wait(barrier, len(greeted))

    def block(d):
        return packed.at[d % 2, :, :, :, pl.ds((d // 2) * piece, piece), :]

    def slot(core, d, where):
        return gathered.at[core, d, :, :, :, pl.ds(where * piece, piece), :]

    def remote(src, dst, send, recv, device):
        return pltpu.make_async_remote_copy(
            src_ref=src, dst_ref=dst, send_sem=send, recv_sem=recv, device_id=device, device_id_type=MESH
        )

    sends = []
    order = (0, 1, 2, 3)
    own, near, sent = {}, {}, {}
    for d in order:
        for k in range(1, gz_n):
            sent[d, k] = remote(
                block(d), slot(gy, d, gz), gz_send.at[k - 1, d], gz_recv.at[k - 1, d], {"gz": side(k)}
            )
            sent[d, k].start()
    edge = {}
    for k in range(gz_n):
        for z in range(z_len):
            for d in range(1, 4):
                row = (d // 2) * piece + z * t_len
                to = (gz * z_len + z) * t_len + t_len - 1
                edge[k, z, d] = remote(
                    packed.at[d % 2, :, :, :, row, :],
                    rim.at[gy, d - 1, :, :, :, to, :],
                    rim_send.at[k, z, d - 1],
                    rim_recv.at[k, z, d - 1],
                    {"ta": earlier, "gz": side(k)},
                )
                edge[k, z, d].start()
    for d in order:
        near[d] = remote(block(d), slot(gy, d, gz), sib_send.at[d], sib_recv.at[d], sibling)
        near[d].start()
        own[d] = pltpu.make_async_copy(block(d), slot(gy, d, gz), own_sem.at[d])
        own[d].start()
    passed = []
    for d in order:
        for k in range(1, gz_n):
            sent[d, k].wait_recv()
            region = slot(gy, d, behind(k))
            copy = remote(region, region, fwd_send.at[k - 1, d], fwd_recv.at[k - 1, d], sibling)
            copy.start()
            passed.append(copy)
    for k in range(gz_n):
        for z in range(z_len):
            for d in range(1, 4):
                edge[k, z, d].wait_recv()
                to = (behind(k) * z_len + z) * t_len + t_len - 1
                region = rim.at[gy, d - 1, :, :, :, to, :]
                copy = remote(region, region, rfw_send.at[k, z, d - 1], rfw_recv.at[k, z, d - 1], sibling)
                copy.start()
                passed.append(copy)
    for d in order:
        own[d].wait()
        near[d].wait()
        for k in range(1, gz_n):
            sent[d, k].wait_send()
    for copy in edge.values():
        copy.wait_send()
    for copy in passed:
        copy.wait()

    full = (rows, LANES)
    row_id = lax.broadcasted_iota(jnp.int32, full, 0)
    lane_id = lax.broadcasted_iota(jnp.int32, full, 1)
    t_pos = row_id % t_len
    first_t, last_t = t_pos == 0, t_pos == t_len - 1
    low = lane_id < 64
    shade = (row_id // t_len + t_pos + lane_id // 8) % 2
    even_x = (shade == 0, shade == 1)
    x_first, x_last = lane_id % 8 == 0, lane_id % 8 == 7

    def choose(mask, a, b):
        shape = a.shape
        return jnp.where(jnp.broadcast_to(mask, shape), a, b)

    def spread(piece_0, piece_1, put):
        for parity in range(2):
            if parity == 0:
                value = choose(low, piece_0, roll(piece_1, 64, 4))
            else:
                value = choose(low, roll(piece_0, 64, 4), piece_1)
            put(parity, closed((value[:, :, 0], value[:, :, 1])))

    for d in range(4):

        def put(parity, pair):
            link_r[parity, d], link_i[parity, d] = pair

        spread(gathered[0, d], gathered[1, d], put)
    for d in range(3):

        def put(parity, pair):
            rim_r[parity, d], rim_i[parity, d] = pair

        spread(rim[0, d], rim[1, d], put)

    def link(d, parity):
        return link_r[parity, d], link_i[parity, d]

    def rim_link(d, parity):
        return rim_r[parity, d - 1], rim_i[parity, d - 1]

    def moved(value, direction, sign, parity):
        sub, lane = value.ndim - 2, value.ndim - 1
        if direction == 0:
            return roll(value, -sign, sub)
        if direction == 1:
            return roll(value, -sign * t_len, sub)
        if direction == 2:
            return roll(value, -sign * 8, lane)
        edge_x = x_last if sign > 0 else x_first
        turned = choose(edge_x, roll(value, sign * 7, lane), roll(value, -sign, lane))
        stays = even_x[parity] if sign > 0 else even_x[1 - parity]
        return choose(stays, value, turned)

    def shifted(pair, direction, sign, parity, beyond=None):
        out = []
        for n in range(2):
            value = moved(pair[n], direction, sign, parity)
            if direction == 0:
                value = choose(last_t if sign > 0 else first_t, beyond[n], value)
            out.append(value)
        return tuple(out)

    def ahead(nu, mu, parity, cut):
        beyond = cut(rim_link(nu, 1 - parity)) if mu == 0 else None
        return shifted(cut(link(nu, 1 - parity)), mu, 1, parity, beyond)

    def upper(mu, nu, parity, beyond=None):
        if nu == 0:
            across = closed(shifted(two_rows(link(mu, 1 - parity)), 0, 1, parity, beyond))
        else:
            across = shifted(link(mu, 1 - parity), nu, 1, parity)
        part = product(ahead(nu, mu, parity, two_rows), across, b_dagger=True)
        return product(part, link(nu, parity), b_dagger=True)

    def lower(mu, nu, parity):
        part = product(link(mu, parity), ahead(nu, mu, parity, two_columns))
        return product(part, link(nu, parity), a_dagger=True)

    def both(mu, nu, parity):
        up = closed(upper(mu, nu, parity))
        down = closed(shifted(lower(mu, nu, 1 - parity), nu, -1, parity))
        return plus(up, down)

    def renew(mu, parity, staple):
        link_r[parity, mu], link_i[parity, mu] = reflect(link(mu, parity), staple)

    messages = []

    def send_up(n, pair):
        up_out[n] = choose(first_t, roll(pair[0], -1, 2), pair[1])
        copy = remote(up_out.at[n], up_in.at[n], up_send.at[n], up_recv.at[n], {"ta": later})
        copy.start()
        messages.append(copy)
        return copy

    def send_down(n, pair):
        down_out[n] = choose(first_t, pair[0], roll(pair[1], 1, 2))
        copy = remote(down_out.at[n], down_in.at[n], down_send.at[n], down_recv.at[n], {"ta": earlier})
        copy.start()
        messages.append(copy)
        return copy

    stores = []
    row_natural = (row_id // t_len + t_pos + lane_id // X + lane_id % X) % 2
    back = (lane_id // X) * 8 + (lane_id % X) // 2 + 64 * row_natural

    def write(d):
        for i in range(3):
            for j in range(3):
                for c, ref in enumerate((link_r, link_i)):
                    zero = jnp.where(gy == 0, ref[0, d, i, j], roll(ref[0, d, i, j], 64, 1))
                    one = jnp.where(gy == 0, roll(ref[1, d, i, j], 64, 1), ref[1, d, i, j])
                    natural[d, i, j, c] = jnp.take_along_axis(jnp.where(low, zero, one), back, axis=1)
        for z in range(z_len):
            for t in range(t_len):
                copy = pltpu.make_async_copy(
                    natural.at[d, :, :, :, gz * piece + z * t_len + t, :],
                    o_ref.at[d, :, :, :, t, z, :],
                    store_sem.at[d, z * t_len + t],
                )
                copy.start()
                stores.append(copy)

    for parity in range(2):
        total = both(0, 1, parity)
        for nu in (2, 3):
            total = plus(total, both(0, nu, parity))
        renew(0, parity, total)

    back_loop, from_below = {}, {}
    for mu in (1, 2, 3):
        back_loop[mu] = lower(mu, 0, 1)
        from_below[mu] = send_up(mu - 1, back_loop[mu])
    write(0)

    def arrived(n):
        value = up_in[n]
        return value, roll(value, -1, 2)

    def time_part(mu, parity, ahead_rows, behind_loop, n):
        up = closed(upper(mu, 0, parity, ahead_rows))
        down = closed(shifted(behind_loop, 0, -1, parity, arrived(n)))
        return plus(up, down)

    for mu in (1, 2, 3):
        others = [nu for nu in (1, 2, 3) if nu != mu]
        total = plus(both(mu, others[0], 0), both(mu, others[1], 0))
        from_below[mu].wait_recv()
        total = plus(total, time_part(mu, 0, two_rows(rim_link(mu, 1)), back_loop[mu], mu - 1))
        renew(mu, 0, total)
        n = 2 + mu
        from_above = send_down(mu - 1, two_rows(link(mu, 0)))
        new_loop = lower(mu, 0, 0)
        below = send_up(n, new_loop)
        total = plus(both(mu, others[0], 1), both(mu, others[1], 1))
        from_above.wait_recv()
        value = down_in[mu - 1]
        ahead_rows = (roll(value, 1, 2), value)
        below.wait_recv()
        total = plus(total, time_part(mu, 1, ahead_rows, new_loop, n))
        renew(mu, 1, total)
        write(mu)

    for copy in messages:
        copy.wait_send()
    for copy in stores:
        copy.wait()


def on_device(counts, raw_links):
    ta_n, gz_n = counts
    t_len, z_len, lanes = raw_links.shape[4:]
    assert t_len == 2 and z_len % 2 == 0 and lanes == LANES
    piece = t_len * z_len
    rows = gz_n * piece
    f32 = jnp.float32
    dma = pltpu.SemaphoreType.DMA
    side = max(gz_n - 1, 1)
    return pl.pallas_call(
        functools.partial(kernel, (ta_n, gz_n, t_len, z_len)),
        out_shape=jax.ShapeDtypeStruct(raw_links.shape, f32),
        in_specs=[pl.BlockSpec(memory_space=pl.ANY)],
        out_specs=pl.BlockSpec(memory_space=pl.ANY),
        scratch_shapes=[
            pltpu.VMEM((2, 2, 3, 2, 2 * piece, LANES), f32),
            pltpu.VMEM((2, 2, 3, 2, 2 * piece, LANES), f32),
            pltpu.VMEM((2, 4, 2, 3, 2, rows, LANES), f32),
            pltpu.VMEM((2, 3, 2, 3, 2, rows, LANES), f32),
            pltpu.VMEM((2, 4, 3, 3, rows, LANES), f32),
            pltpu.VMEM((2, 4, 3, 3, rows, LANES), f32),
            pltpu.VMEM((2, 3, 3, 3, rows, LANES), f32),
            pltpu.VMEM((2, 3, 3, 3, rows, LANES), f32),
            pltpu.VMEM((6, 2, 3, rows, LANES), f32),
            pltpu.VMEM((6, 2, 3, rows, LANES), f32),
            pltpu.VMEM((3, 2, 3, rows, LANES), f32),
            pltpu.VMEM((3, 2, 3, rows, LANES), f32),
            pltpu.VMEM((4, 3, 3, 2, rows, LANES), f32),
            dma((2 * piece,)),
            dma((4,)),
            dma((4,)),
            dma((4,)),
            dma((side, 4)),
            dma((side, 4)),
            dma((side, 4)),
            dma((side, 4)),
            dma((gz_n, z_len, 3)),
            dma((gz_n, z_len, 3)),
            dma((gz_n, z_len, 3)),
            dma((gz_n, z_len, 3)),
            dma((6,)),
            dma((6,)),
            dma((3,)),
            dma((3,)),
            dma((4, piece)),
        ],
        compiler_params=pltpu.CompilerParams(
            collective_id=0, has_side_effects=True, vmem_limit_bytes=32 * 1024 * 1024
        ),
    )(raw_links)


def solution(mesh):
    spec = P("ens", None, None, None, "ta", "gz", "gy")
    assert mesh.shape["gy"] == 2
    return jax.shard_map(
        functools.partial(on_device, (mesh.shape["ta"], mesh.shape["gz"])),
        mesh=mesh,
        in_specs=(spec,),
        out_specs=spec,
        check_vma=False,
    )
```

profile of v0, /device:TPU:0, one launch (start us, length us, event | category | flops | bytes accessed | tf_op | source)
XLA Modules:
  0.0 30.9 jit_solution(1526000075470242535)
XLA Ops:
  0.0 0.0 copy-start
  0.0 0.9 %copy-done = f32[4,3,3,2,2,2,128]{6,5,4,3,2,1,0:T(2,128)S(1)} copy-done((f32[4,3,3,2,2,2,128]{6,5,4,3,2,1,0:T(2,128)S(1)}, f32[4,3,3,2,2,2,128]{6,5,4,3,2,1,0:T(2,128)}, u32[]{:S(2)}) %copy-start) | copy-done | bytes 147480
  0.9 29.3 %shard_map.17 = f32[4,3,3,2,2,2,128]{6,5,4,3,2,1,0:T(2,128)S(1)} custom-call(f32[4,3,3,2,2,2,128]{6,5,4,3,2,1,0:T(2,128)S(1)} %copy-done), custom_call_target="tpu_custom_call" | custom-call | tf_op jit(solution)/shard_map/pallas_call | solution.py:469
  30.2 0.7 %copy.3 = f32[4,3,3,2,2,2,128]{6,5,4,3,2,1,0:T(2,128)} copy(f32[4,3,3,2,2,2,128]{6,5,4,3,2,1,0:T(2,128)S(1)} %shard_map.17) | data formatting | bytes 294912
Async XLA Ops:
  0.0 0.9 %copy-start = (f32[4,3,3,2,2,2,128]{6,5,4,3,2,1,0:T(2,128)S(1)}, f32[4,3,3,2,2,2,128]{6,5,4,3,2,1,0:T(2,128)}, u32[]{:S(2)}) copy-start(f32[4,3,3,2,2,2,128]{6,5,4,3,2,1,0:T(2,128)} %x_ref.1) | copy-start | bytes 442372
where the time goes:
time: 31 us; the launch traced here: 30.9 us
  Pallas kernels  29.3 us (95%)
  local copies, waits for them, and re-layouts  1.57 us (5%)
    pallas_call x1, Pallas kernels, on_device(): pl.pallas_call(functools.partial(kernel, (ta_n, gz_n, t_len, z_len)), out...  29.3 us
    unnamed x3, local copies, waits for them, and re-layouts  1.57 us

commit v1 on v0

--- a/solution.py
+++ b/solution.py
@@ -138,6 +138,7 @@
     o_ref,
     raw,
     packed,
+    edging,
     gathered,
     rim,
     link_r,
@@ -219,73 +220,83 @@
                 for c in range(2):
                     packed[pair, i, j, c] = jnp.take_along_axis(entry[c], pick, axis=1)
 
+    early_row = row_id % t_len == 0
+    for pair in range(2):
+        for i in range(2):
+            for j in range(3):
+                real, imag = packed[pair, i, j, 0], packed[pair, i, j, 1]
+                edging[0, pair, i, j] = jnp.where(early_row, real, roll(imag, 1, 0))
+                edging[1, pair, i, j] = jnp.where(early_row, roll(real, -1, 0), imag)
+
     pl.semaphore_wait(barrier, len(greeted))
 
-    def block(d):
-        return packed.at[d % 2, :, :, :, pl.ds((d // 2) * piece, piece), :]
-
-    def slot(core, d, where):
-        return gathered.at[core, d, :, :, :, pl.ds(where * piece, piece), :]
+    def block(half):
+        return packed.at[:, :, :, :, pl.ds(half * piece, piece), :]
+
+    def slot(core, half, where):
+        return gathered.at[core, 2 * half : 2 * half + 2, :, :, :, pl.ds(where * piece, piece), :]
 
     def remote(src, dst, send, recv, device):
         return pltpu.make_async_remote_copy(
             src_ref=src, dst_ref=dst, send_sem=send, recv_sem=recv, device_id=device, device_id_type=MESH
         )
 
-    sends = []
-    order = (0, 1, 2, 3)
-    own, near, sent = {}, {}, {}
-    for d in order:
+    def edge_slot(side_of, half, core, where):
+        first = 1 if side_of == 0 and half == 0 else 2 * half
+        return rim.at[core, side_of, first : 2 * half + 2, :, :, pl.ds(where * piece, piece), :]
+
+    halves = (0, 1)
+    own, near, sent, edge = {}, {}, {}, {}
+    for half in halves:
         for k in range(1, gz_n):
-            sent[d, k] = remote(
-                block(d), slot(gy, d, gz), gz_send.at[k - 1, d], gz_recv.at[k - 1, d], {"gz": side(k)}
+            copy = remote(
+                block(half),
+                slot(gy, half, gz),
+                gz_send.at[k - 1, half],
+                gz_recv.at[k - 1, half],
+                {"gz": side(k)},
             )
-            sent[d, k].start()
-    edge = {}
-    for k in range(gz_n):
-        for z in range(z_len):
-            for d in range(1, 4):
-                row = (d // 2) * piece + z * t_len
-                to = (gz * z_len + z) * t_len + t_len - 1
-                edge[k, z, d] = remote(
-                    packed.at[d % 2, :, :, :, row, :],
-                    rim.at[gy, d - 1, :, :, :, to, :],
-                    rim_send.at[k, z, d - 1],
-                    rim_recv.at[k, z, d - 1],
-                    {"ta": earlier, "gz": side(k)},
-                )
-                edge[k, z, d].start()
-    for d in order:
-        near[d] = remote(block(d), slot(gy, d, gz), sib_send.at[d], sib_recv.at[d], sibling)
-        near[d].start()
-        own[d] = pltpu.make_async_copy(block(d), slot(gy, d, gz), own_sem.at[d])
-        own[d].start()
-    passed = []
-    for d in order:
+            copy.start()
+            sent[half, k] = copy
+    edges = [(k, side_of, half) for k in reversed(range(gz_n)) for side_of in range(2) for half in halves]
+    for k, side_of, half in edges:
+        first = 1 if side_of == 0 and half == 0 else 0
+        copy = remote(
+            edging.at[side_of, first:2, :, :, pl.ds(half * piece, piece), :],
+            edge_slot(side_of, half, gy, gz),
+            rim_send.at[k, side_of, half],
+            rim_recv.at[k, side_of, half],
+            {"ta": later if side_of else earlier, "gz": side(k)},
+        )
+        copy.start()
+        edge[k, side_of, half] = copy
+    for half in halves:
+        near[half] = remote(block(half), slot(gy, half, gz), sib_send.at[half], sib_recv.at[half], sibling)
+        near[half].start()
+        own[half] = pltpu.make_async_copy(block(half), slot(gy, half, gz), own_sem.at[half])
+        own[half].start()
+    passed, passed_edges = [], []
+    for half in halves:
         for k in range(1, gz_n):
-            sent[d, k].wait_recv()
-            region = slot(gy, d, behind(k))
-            copy = remote(region, region, fwd_send.at[k - 1, d], fwd_recv.at[k - 1, d], sibling)
+            sent[half, k].wait_recv()
+            region = slot(gy, half, behind(k))
+            copy = remote(region, region, fwd_send.at[k - 1, half], fwd_recv.at[k - 1, half], sibling)
             copy.start()
             passed.append(copy)
-    for k in range(gz_n):
-        for z in range(z_len):
-            for d in range(1, 4):
-                edge[k, z, d].wait_recv()
-                to = (behind(k) * z_len + z) * t_len + t_len - 1
-                region = rim.at[gy, d - 1, :, :, :, to, :]
-                copy = remote(region, region, rfw_send.at[k, z, d - 1], rfw_recv.at[k, z, d - 1], sibling)
-                copy.start()
-                passed.append(copy)
-    for d in order:
-        own[d].wait()
-        near[d].wait()
-        for k in range(1, gz_n):
-            sent[d, k].wait_send()
-    for copy in edge.values():
-        copy.wait_send()
-    for copy in passed:
-        copy.wait()
+
+    def pass_edges():
+        for k, side_of, half in reversed(edges):
+            edge[k, side_of, half].wait_recv()
+            region = edge_slot(side_of, half, gy, behind(k))
+            copy = remote(
+                region,
+                region,
+                rfw_send.at[k, side_of, half],
+                rfw_recv.at[k, side_of, half],
+                sibling,
+            )
+            copy.start()
+            passed_edges.append(copy)
 
     full = (rows, LANES)
     row_id = lax.broadcasted_iota(jnp.int32, full, 0)
@@ -309,21 +320,42 @@
                 value = choose(low, roll(piece_0, 64, 4), piece_1)
             put(parity, closed((value[:, :, 0], value[:, :, 1])))
 
+    for half in halves:
+        own[half].wait()
+        near[half].wait()
+        for k in range(1, gz_n):
+            sent[half, k].wait_send()
+    for copy in passed:
+        copy.wait()
     for d in range(4):
 
         def put(parity, pair):
-            link_r[parity, d], link_i[parity, d] = pair
+            link_r[0, parity, d], link_i[0, parity, d] = pair
 
         spread(gathered[0, d], gathered[1, d], put)
-    for d in range(3):
+    def unfolded(value):
+        return jnp.stack([roll(value, 1, 2), value], axis=2)
+
+    pass_edges()
+    for copy in edge.values():
+        copy.wait_send()
+    for copy in passed_edges:
+        copy.wait()
+    for d in range(1, 4):
 
         def put(parity, pair):
-            rim_r[parity, d], rim_i[parity, d] = pair
-
-        spread(rim[0, d], rim[1, d], put)
-
-    def link(d, parity):
-        return link_r[parity, d], link_i[parity, d]
+            rim_r[parity, d - 1], rim_i[parity, d - 1] = pair
+
+        spread(unfolded(rim[0, 0, d]), unfolded(rim[1, 0, d]), put)
+    for d in range(4):
+
+        def put(parity, pair):
+            link_r[1, parity, d], link_i[1, parity, d] = pair
+
+        spread(unfolded(rim[0, 1, d]), unfolded(rim[1, 1, d]), put)
+
+    def link(d, parity, at=0):
+        return link_r[at, parity, d], link_i[at, parity, d]
 
     def rim_link(d, parity):
         return rim_r[parity, d - 1], rim_i[parity, d - 1]
@@ -350,29 +382,34 @@
             out.append(value)
         return tuple(out)
 
-    def ahead(nu, mu, parity, cut):
-        beyond = cut(rim_link(nu, 1 - parity)) if mu == 0 else None
-        return shifted(cut(link(nu, 1 - parity)), mu, 1, parity, beyond)
-
-    def upper(mu, nu, parity, beyond=None):
+    def ahead(nu, mu, parity, cut, at):
+        beyond = None
+        if mu == 0 and at == 0:
+            beyond = cut(rim_link(nu, 1 - parity))
+        elif mu == 0:
+            beyond = tuple(roll(part, 1, 2) for part in cut(link(nu, 1 - parity)))
+        return shifted(cut(link(nu, 1 - parity, at)), mu, 1, parity, beyond)
+
+    def upper(mu, nu, parity, at=0, beyond=None):
         if nu == 0:
             across = closed(shifted(two_rows(link(mu, 1 - parity)), 0, 1, parity, beyond))
         else:
-            across = shifted(link(mu, 1 - parity), nu, 1, parity)
-        part = product(ahead(nu, mu, parity, two_rows), across, b_dagger=True)
-        return product(part, link(nu, parity), b_dagger=True)
-
-    def lower(mu, nu, parity):
-        part = product(link(mu, parity), ahead(nu, mu, parity, two_columns))
-        return product(part, link(nu, parity), a_dagger=True)
-
-    def both(mu, nu, parity):
-        up = closed(upper(mu, nu, parity))
-        down = closed(shifted(lower(mu, nu, 1 - parity), nu, -1, parity))
+            across = shifted(link(mu, 1 - parity, at), nu, 1, parity)
+        part = product(ahead(nu, mu, parity, two_rows, at), across, b_dagger=True)
+        return product(part, link(nu, parity, at), b_dagger=True)
+
+    def lower(mu, nu, parity, at=0):
+        part = product(link(mu, parity, at), ahead(nu, mu, parity, two_columns, at))
+        return product(part, link(nu, parity, at), a_dagger=True)
+
+    def both(mu, nu, parity, at=0):
+        up = closed(upper(mu, nu, parity, at))
+        down = closed(shifted(lower(mu, nu, 1 - parity, at), nu, -1, parity))
         return plus(up, down)
 
-    def renew(mu, parity, staple):
-        link_r[parity, mu], link_i[parity, mu] = reflect(link(mu, parity), staple)
+    def renew(mu, parity, staple, at=0):
+        new = reflect(link(mu, parity, at), staple)
+        link_r[at, parity, mu], link_i[at, parity, mu] = new
 
     messages = []
 
@@ -398,8 +435,8 @@
         for i in range(3):
             for j in range(3):
                 for c, ref in enumerate((link_r, link_i)):
-                    zero = jnp.where(gy == 0, ref[0, d, i, j], roll(ref[0, d, i, j], 64, 1))
-                    one = jnp.where(gy == 0, roll(ref[1, d, i, j], 64, 1), ref[1, d, i, j])
+                    zero = jnp.where(gy == 0, ref[0, 0, d, i, j], roll(ref[0, 0, d, i, j], 64, 1))
+                    one = jnp.where(gy == 0, roll(ref[0, 1, d, i, j], 64, 1), ref[0, 1, d, i, j])
                     natural[d, i, j, c] = jnp.take_along_axis(jnp.where(low, zero, one), back, axis=1)
         for z in range(z_len):
             for t in range(t_len):
@@ -412,44 +449,49 @@
                 stores.append(copy)
 
     for parity in range(2):
-        total = both(0, 1, parity)
-        for nu in (2, 3):
-            total = plus(total, both(0, nu, parity))
-        renew(0, parity, total)
-
-    back_loop, from_below = {}, {}
-    for mu in (1, 2, 3):
-        back_loop[mu] = lower(mu, 0, 1)
-        from_below[mu] = send_up(mu - 1, back_loop[mu])
-    write(0)
-
-    def arrived(n):
-        value = up_in[n]
-        return value, roll(value, -1, 2)
-
-    def time_part(mu, parity, ahead_rows, behind_loop, n):
-        up = closed(upper(mu, 0, parity, ahead_rows))
-        down = closed(shifted(behind_loop, 0, -1, parity, arrived(n)))
+        for at in range(2):
+            total = both(0, 1, parity, at)
+            for nu in (2, 3):
+                total = plus(total, both(0, nu, parity, at))
+            renew(0, parity, total, at)
+
+    def upward(pair):
+        return tuple(roll(part, -1, 2) for part in pair)
+
+    def time_part(mu, parity, ahead_rows, behind_loop, beyond):
+        up = closed(upper(mu, 0, parity, 0, ahead_rows))
+        down = closed(shifted(behind_loop, 0, -1, parity, beyond))
         return plus(up, down)
 
+    def time_start(mu):
+        return time_part(mu, 0, two_rows(rim_link(mu, 1)), lower(mu, 0, 1), upward(lower(mu, 0, 1, 1)))
+
+    total = plus(plus(both(1, 2, 0), both(1, 3, 0)), time_start(1))
     for mu in (1, 2, 3):
         others = [nu for nu in (1, 2, 3) if nu != mu]
-        total = plus(both(mu, others[0], 0), both(mu, others[1], 0))
-        from_below[mu].wait_recv()
-        total = plus(total, time_part(mu, 0, two_rows(rim_link(mu, 1)), back_loop[mu], mu - 1))
         renew(mu, 0, total)
-        n = 2 + mu
         from_above = send_down(mu - 1, two_rows(link(mu, 0)))
         new_loop = lower(mu, 0, 0)
-        below = send_up(n, new_loop)
+        below = send_up(mu - 1, new_loop)
         total = plus(both(mu, others[0], 1), both(mu, others[1], 1))
+        if mu == 1:
+            write(0)
+            early = {2: plus(both(2, 3, 0), time_start(2)), 3: time_start(3)}
+        if mu == 2:
+            write(1)
+            early[3] = plus(early[3], both(3, 1, 0))
+        if mu == 3:
+            write(2)
         from_above.wait_recv()
         value = down_in[mu - 1]
         ahead_rows = (roll(value, 1, 2), value)
         below.wait_recv()
-        total = plus(total, time_part(mu, 1, ahead_rows, new_loop, n))
+        value = up_in[mu - 1]
+        total = plus(total, time_part(mu, 1, ahead_rows, new_loop, (value, roll(value, -1, 2))))
         renew(mu, 1, total)
-        write(mu)
+        if mu < 3:
+            total = plus(early[mu + 1], both(mu + 1, mu, 0))
+    write(3)
 
     for copy in messages:
         copy.wait_send()
@@ -469,36 +511,37 @@
     return pl.pallas_call(
         functools.partial(kernel, (ta_n, gz_n, t_len, z_len)),
         out_shape=jax.ShapeDtypeStruct(raw_links.shape, f32),
-        in_specs=[pl.BlockSpec(memory_space=pl.ANY)],
+        in_specs=[pl.BlockSpec(memory_space=pltpu.HBM)],
         out_specs=pl.BlockSpec(memory_space=pl.ANY),
         scratch_shapes=[
             pltpu.VMEM((2, 2, 3, 2, 2 * piece, LANES), f32),
             pltpu.VMEM((2, 2, 3, 2, 2 * piece, LANES), f32),
+            pltpu.VMEM((2, 2, 2, 3, 2 * piece, LANES), f32),
             pltpu.VMEM((2, 4, 2, 3, 2, rows, LANES), f32),
-            pltpu.VMEM((2, 3, 2, 3, 2, rows, LANES), f32),
-            pltpu.VMEM((2, 4, 3, 3, rows, LANES), f32),
-            pltpu.VMEM((2, 4, 3, 3, rows, LANES), f32),
+            pltpu.VMEM((2, 2, 4, 2, 3, rows, LANES), f32),
+            pltpu.VMEM((2, 2, 4, 3, 3, rows, LANES), f32),
+            pltpu.VMEM((2, 2, 4, 3, 3, rows, LANES), f32),
             pltpu.VMEM((2, 3, 3, 3, rows, LANES), f32),
             pltpu.VMEM((2, 3, 3, 3, rows, LANES), f32),
-            pltpu.VMEM((6, 2, 3, rows, LANES), f32),
-            pltpu.VMEM((6, 2, 3, rows, LANES), f32),
+            pltpu.VMEM((3, 2, 3, rows, LANES), f32),
+            pltpu.VMEM((3, 2, 3, rows, LANES), f32),
             pltpu.VMEM((3, 2, 3, rows, LANES), f32),
             pltpu.VMEM((3, 2, 3, rows, LANES), f32),
             pltpu.VMEM((4, 3, 3, 2, rows, LANES), f32),
             dma((2 * piece,)),
-            dma((4,)),
-            dma((4,)),
-            dma((4,)),
-            dma((side, 4)),
-            dma((side, 4)),
-            dma((side, 4)),
-            dma((side, 4)),
-            dma((gz_n, z_len, 3)),
-            dma((gz_n, z_len, 3)),
-            dma((gz_n, z_len, 3)),
-            dma((gz_n, z_len, 3)),
-            dma((6,)),
-            dma((6,)),
+            dma((2,)),
+            dma((2,)),
+            dma((2,)),
+            dma((side, 2)),
+            dma((side, 2)),
+            dma((side, 2)),
+            dma((side, 2)),
+            dma((gz_n, 2, 2)),
+            dma((gz_n, 2, 2)),
+            dma((gz_n, 2, 2)),
+            dma((gz_n, 2, 2)),
+            dma((3,)),
+            dma((3,)),
             dma((3,)),
             dma((3,)),
             dma((4, piece)),

time: 31 us -> 30.4 us (0.981)
  Pallas kernels: 29.3 us -> 28.6 us
    pallas_call x1, Pallas kernels: 29.3 us -> 28.6 us  [on_device(): pl.pallas_call(functools.partial(kernel, (ta_n, gz_n, t_len, z_len)), out...]
where the time goes in v1:
time: 30.4 us; the launch traced here: 30.2 us
  Pallas kernels  28.6 us (94%)
  local copies, waits for them, and re-layouts  1.57 us (5%)
    pallas_call x1, Pallas kernels, on_device(): pl.pallas_call(functools.partial(kernel, (ta_n, gz_n, t_len, z_len)), out...  28.6 us
    unnamed x3, local copies, waits for them, and re-layouts  1.57 us

profile of v1, /device:TPU:0, one launch (start us, length us, event | category | flops | bytes accessed | tf_op | source)
XLA Modules:
  0.0 30.2 jit_solution(59362111809546759)
XLA Ops:
  0.0 0.0 copy-start
  0.0 0.9 %copy-done = f32[4,3,3,2,2,2,128]{6,5,4,3,2,1,0:T(2,128)S(1)} copy-done((f32[4,3,3,2,2,2,128]{6,5,4,3,2,1,0:T(2,128)S(1)}, f32[4,3,3,2,2,2,128]{6,5,4,3,2,1,0:T(2,128)}, u32[]{:S(2)}) %copy-start) | copy-done | bytes 147480
  0.9 28.6 %shard_map.17 = f32[4,3,3,2,2,2,128]{6,5,4,3,2,1,0:T(2,128)S(1)} custom-call(f32[4,3,3,2,2,2,128]{6,5,4,3,2,1,0:T(2,128)S(1)} %copy-done), custom_call_target="tpu_custom_call" | custom-call | tf_op jit(solution)/shard_map/pallas_call | solution.py:511
  29.6 0.7 %copy.3 = f32[4,3,3,2,2,2,128]{6,5,4,3,2,1,0:T(2,128)} copy(f32[4,3,3,2,2,2,128]{6,5,4,3,2,1,0:T(2,128)S(1)} %shard_map.17) | data formatting | bytes 294912
Async XLA Ops:
  0.0 0.9 %copy-start = (f32[4,3,3,2,2,2,128]{6,5,4,3,2,1,0:T(2,128)S(1)}, f32[4,3,3,2,2,2,128]{6,5,4,3,2,1,0:T(2,128)}, u32[]{:S(2)}) copy-start(f32[4,3,3,2,2,2,128]{6,5,4,3,2,1,0:T(2,128)} %x_ref.1) | copy-start | bytes 442372
